TPU v7x, 32 devices: a whole 2x2x4 slice. The times are simulated.
32 devices in a mesh: ctx: 2 (over core), exp: 4 (over y, x), req: 4 (over z).
Axes of the slice: x: 2, y: 2, z: 4, core: 2. Of those that a mesh axis runs over, the one named last changes fastest.
Arguments:
- queries: bfloat16 [64, 2, 128, 576], P('req', None, ('ctx', 'exp')), parts along dimension 0, may hold values from -21 to 21
- latent_cache: bfloat16 [64, 4096, 576], P('req', ('ctx', 'exp')), parts along dimension 0, may hold values from -4 to 4
- context_lengths: int32 [64], P('req'), parts along dimension 0, may hold values from 16 to 4095, as said below
- value_up: bfloat16 [128, 512, 128], P(('ctx', 'exp')), may hold values from -0.25 to 0.25
- out_proj: bfloat16 [16384, 7168], P(('ctx', 'exp')), may hold values from -0.09375 to 0.09375
- residual: bfloat16 [128, 7168], P(('req', 'exp')), parts along dimension 0, may hold values from -3 to 3
- norm_gain: bfloat16 [7168], replicated, may hold values from 0.099609375 to 1.8984375
- router: bfloat16 [7168, 4], replicated, may hold values from -0.125 to 0.125
- routes: int32 [128, 2], P(('req', 'exp')), parts along dimension 0, may hold values from 0 to 3, all different within a row; in each aligned block of 8 rows (0 to 7, 8 to 15, ...) at most 4 rows name the same one
- expert_gate: bfloat16 [4, 7168, 1024], P('exp', None, 'ctx'), may hold values from -0.0625 to 0.0625
- expert_up: bfloat16 [4, 7168, 1024], P('exp', None, 'ctx'), may hold values from -0.0625 to 0.0625
- expert_down: bfloat16 [4, 1024, 7168], P('exp', 'ctx'), may hold values from -0.375 to 0.375
Outputs:
- output: bfloat16 [128, 7168], P(('req', 'exp'), 'ctx'), parts along dimension 0
There are 4 independent parts, one for each index of `req`. A program takes and returns all parts, laid end to end along the dimension named above; an argument that names none is the same for every part. Nothing has to cross between parts.
Inputs may be any that keep to these rules, and one draw needn't show every extreme that they name: Verify row j of request r sees context positions below context_lengths[r] + j; in every draw one request has 4095. `routes`: each row names 2 different experts; in each aligned block of 8 rows (the rows of one index of exp) no expert is named by more than 4 rows.
All inputs are finite; a program needn't handle non-finite values.
Results may differ from a plain program's by a relative error of at most 0.028.
Values may be sent and summed in bfloat16 or wider, within the bound.
A program may use at most 128 MiB of HBM per device.

v0:
```python
import functools
import math

import jax
import jax.numpy as jnp
from jax import lax
from jax.experimental import pallas as pl
from jax.experimental.pallas import tpu as pltpu
from jax.sharding import PartitionSpec as P

route_scale = 2.5


def on_device(
    queries,
    latent_cache,
    context_lengths,
    value_up,
    out_proj,
    residual,
    norm_gain,
    router,
    routes,
    expert_gate,
    expert_up,
    expert_down,
):
    latent_width = value_up.shape[1]
    value_width = value_up.shape[2]
    rope_width = queries.shape[3] - latent_width
    score_scale = 1.0 / math.sqrt(value_width + rope_width)
    heads_here = queries.shape[2]
    block_len = latent_cache.shape[1]
    device = lax.axis_index(("ctx", "exp"))
    all_queries = lax.all_gather(queries, ("ctx", "exp"), axis=2, tiled=True)
    scores = (
        jnp.einsum("rjhd,rtd->rjht", all_queries, latent_cache, preferred_element_type=jnp.float32)
        * score_scale
    )
    positions = device * block_len + jnp.arange(block_len, dtype=jnp.int32)
    visible_upto = context_lengths[:, None] + jnp.arange(2, dtype=jnp.int32)[None, :]
    visible = positions[None, None, None, :] < visible_upto[:, :, None, None]
    masked = jnp.where(visible, scores, -1e30)
    row_max = lax.pmax(jnp.max(masked, axis=-1), ("ctx", "exp"))
    weights = jnp.where(visible, jnp.exp(masked - row_max[..., None]), 0.0)
    weight_sum = jnp.sum(weights, axis=-1)
    latents = latent_cache[:, :, :latent_width]
    weighted = jnp.einsum(
        "rjht,rtl->rjhl", weights.astype(jnp.bfloat16), latents, preferred_element_type=jnp.float32
    )
    summed, sum_all = lax.psum((weighted, weight_sum), ("ctx", "exp"))
    own_weighted = lax.dynamic_slice_in_dim(summed, device * heads_here, heads_here, 2)
    own_sum = lax.dynamic_slice_in_dim(sum_all, device * heads_here, heads_here, 2)
    context = (own_weighted / own_sum[..., None]).astype(jnp.bfloat16)
    head_out = jnp.einsum(
        "rjhl,hlv->rjhv", context, value_up, preferred_element_type=jnp.float32
    ).astype(jnp.bfloat16)
    row_total = head_out.shape[0] * head_out.shape[1]
    head_out = head_out.reshape(row_total, heads_here * value_width)
    own_rows = residual.shape[0]
    owner_index = lax.axis_index("exp")
    attention_all = lax.psum(
        jnp.dot(head_out, out_proj, preferred_element_type=jnp.float32), ("ctx", "exp")
    )
    attention = lax.dynamic_slice_in_dim(attention_all, owner_index * own_rows, own_rows, 0)
    hidden = (residual.astype(jnp.float32) + attention).astype(jnp.bfloat16)
    hidden_wide = hidden.astype(jnp.float32)
    inverse = lax.rsqrt(jnp.mean(hidden_wide * hidden_wide, axis=-1, keepdims=True) + 1e-06)
    normed = (hidden_wide * inverse * norm_gain.astype(jnp.float32)).astype(jnp.bfloat16)
    affinity = jax.nn.sigmoid(jnp.dot(normed, router, preferred_element_type=jnp.float32))
    expert_count = router.shape[1]
    top_count = routes.shape[1]
    capacity = max(2, own_rows * top_count // expert_count)
    chosen = (
        routes[:, :, None] == jnp.arange(expert_count, dtype=jnp.int32)[None, None, :]
    ).astype(jnp.float32)
    picked = jnp.sum(chosen * affinity[:, None, :], axis=-1)
    gate_weights = route_scale * picked / jnp.sum(picked, axis=-1, keepdims=True)
    per_row = jnp.sum(chosen, axis=1)
    earlier = jnp.cumsum(per_row, axis=0) - per_row
    slot_index = jnp.sum(chosen * earlier[:, None, :], axis=-1)
    slot_hot = (
        slot_index[:, :, None] == jnp.arange(capacity, dtype=jnp.float32)[None, None, :]
    ).astype(jnp.float32)
    placement = chosen[:, :, :, None] * slot_hot[:, :, None, :]
    row_place = jnp.sum(placement, axis=1).reshape(own_rows, expert_count * capacity)
    gate_place = jnp.sum(placement * gate_weights[:, :, None, None], axis=1).reshape(
        own_rows, expert_count * capacity
    )
    model_width = normed.shape[1]
    outgoing = jnp.einsum(
        "rs,rd->sd", row_place.astype(jnp.bfloat16), normed, preferred_element_type=jnp.float32
    ).astype(jnp.bfloat16)
    outgoing = outgoing.reshape(expert_count, capacity, model_width)
    arrived = lax.all_to_all(outgoing, "exp", split_axis=0, concat_axis=0, tiled=True)
    gate_part = jnp.einsum(
        "scd,df->scf", arrived, expert_gate[0], preferred_element_type=jnp.float32
    )
    up_part = jnp.einsum("scd,df->scf", arrived, expert_up[0], preferred_element_type=jnp.float32)
    active = (jax.nn.silu(gate_part) * up_part).astype(jnp.bfloat16)
    partial_out = jnp.einsum(
        "scf,fd->scd", active, expert_down[0], preferred_element_type=jnp.float32
    )
    col_width = model_width // lax.axis_size("ctx")
    ctx_index = lax.axis_index("ctx")
    own_cols = lax.dynamic_slice_in_dim(hidden_wide, ctx_index * col_width, col_width, 1)
    full_sum = lax.psum(partial_out.astype(jnp.bfloat16), "ctx").astype(jnp.float32)
    returned = lax.all_to_all(
        full_sum.astype(jnp.bfloat16), "exp", split_axis=0, concat_axis=0, tiled=True
    ).astype(full_sum.dtype)
    returned = lax.dynamic_slice_in_dim(returned, ctx_index * col_width, col_width, 2)
    mixture = jnp.dot(
        gate_place,
        returned.reshape(expert_count * capacity, col_width),
        precision=lax.Precision.HIGHEST,
    )
    return (own_cols + mixture).astype(jnp.bfloat16)


MESH = pl.DeviceIdType.MESH
F32 = jnp.float32
BF16 = jnp.bfloat16
PAIR = 2
SLOTS = 5
BLOCKS = 8
AHEAD = 3


def lay_out(chunks):
    places, count = {}, 0
    for name, number in (
        ("own", 3), ("diag", 2), ("core", 4), ("stat", 7), ("fold", 1), ("cross", 2), ("last", 2),
    ):
        places[name] = (count, number)
        count += number * chunks
    for name, number in (("route", 3), ("swap", 2), ("rows", 6), ("hid", 4), ("hidfwd", 3)):
        places[name] = (count, number)
        count += number
    return places, count


def contract(a, b, da, db):
    return lax.dot_general(a, b, (((da,), (db,)), ((), ())), preferred_element_type=F32)


def layer_kernel(
    lens, q_hbm, cache_hbm, vu_hbm, op_hbm, res, gain, router, routes, eg_hbm, eu_hbm, ed_hbm,
    out,
    qbuf, cbuf, acc, mown, stat, norm, crx, x2, y2, x3, y3, ctx2, vu, ho, wslot, eg, eu,
    sbuf, wbuf, mz, chosen, pbuf, prx, tsum, rrx, hid, xn, act, gcol,
    send, recv, csem, wsem, osem,
):
    chunks, _, heads_rows, width = q_hbm.shape
    heads = heads_rows // 2
    block_len, latent = cache_hbm.shape[3], vu.shape[1]
    vdim = vu.shape[2]
    places, _ = lay_out(chunks)
    scale = 1.0 / math.sqrt(vdim + width - latent)
    half = hid.shape[3]
    cols = half * 2 // BLOCKS
    per_half = BLOCKS // 2
    c = lax.axis_index("ctx")
    e = lax.axis_index("exp")
    ey, ex = e // 2, e % 2
    me = c * 4 + e
    ex_n = e + 1 - 2 * ex
    ey_n = e + 2 - 4 * ey
    ed_n = 3 - e
    others = (ex_n, ey_n, ed_n)
    peers = [(1 - c, e)] + [(c, o) for o in others] + [(1 - c, o) for o in others]

    def remote(kind, g, k, src, dst, to):
        first, stride = places[kind]
        place = first + g * stride + k
        return pltpu.make_async_remote_copy(
            src_ref=src, dst_ref=dst, send_sem=send.at[place], recv_sem=recv.at[place],
            device_id={"ctx": to[0], "exp": to[1]}, device_id_type=MESH,
        )

    core_to, x_to, y_to = (1 - c, e), (c, ex_n), (c, ey_n)

    def own_copy(g, k):
        return remote("own", g, k, q_hbm.at[g], qbuf.at[g, me], (core_to, x_to, y_to)[k])

    def diag_copy(g, k):
        source = c * 4 + (ex_n if k == 0 else ey_n)
        view = qbuf.at[g, source, k]
        return remote("diag", g, k, view, view, (y_to, x_to)[k])

    def core_copy(g, k):
        source = c * 4 + (ex_n, ey_n, ed_n, ed_n)[k]
        view = qbuf.at[g, source] if k < 2 else qbuf.at[g, source, k - 2]
        return remote("core", g, k, view, view, core_to)

    def stat_copy(g, k):
        return remote("stat", g, k, stat.at[g, me], stat.at[g, me], peers[k])

    def fold_copy(g):
        return remote("fold", g, 0, norm.at[g, 1 - c], crx.at[g], core_to)

    def cross_copy(g, k):
        if k == 0:
            return remote("cross", g, 0, crx.at[g, :, 1 - ex, 0], x2.at[g], x_to)
        return remote("cross", g, 1, crx.at[g, 1 - ey, :, 1], y2.at[g], y_to)

    def last_copy(g, k):
        if k == 0:
            return remote("last", g, 0, x2.at[g, 1 - ey], y3.at[g], y_to)
        return remote("last", g, 1, y2.at[g, 1 - ex], x3.at[g], x_to)

    def route_copy(k):
        return remote("route", 0, k, chosen.at[e], chosen.at[e], (c, others[k]))

    def swap_copy(p):
        return remote("swap", 0, p, pbuf.at[p, 0], prx.at[p], core_to)

    def rows_copy(p, k):
        return remote("rows", 0, p * 3 + k, tsum.at[p, others[k]], rrx.at[p, k], (c, others[k]))

    def hid_copy(k):
        to = (x_to, y_to, (c, ed_n), core_to)[k]
        return remote("hid", 0, k, hid.at[e, c], hid.at[e, c], to)

    def hidfwd_copy(k):
        view = hid.at[others[k], c]
        return remote("hidfwd", 0, k, view, view, core_to)

    def cache_copy(g):
        return pltpu.make_async_copy(cache_hbm.at[g], cbuf.at[g % 2], csem.at[g % 2])

    def column(i):
        side = jnp.where(i < per_half, 1 - c, c)
        return pl.multiple_of((side * per_half + i % per_half) * cols, cols)

    def op_copy(i):
        return pltpu.make_async_copy(
            op_hbm.at[:, pl.ds(column(i), cols)], wslot.at[i % SLOTS], osem.at[i % SLOTS]
        )

    depth = ed_hbm.shape[0]

    def down_copy(i):
        place = pl.ds(pl.multiple_of((i % 4) * depth, depth), depth)
        return pltpu.make_async_copy(
            ed_hbm.at[:, pl.ds(column(i), cols)], wslot.at[3 + i // 4, place], wsem.at[4 + i]
        )

    own_q = pltpu.make_async_copy(q_hbm, qbuf.at[:, me], wsem.at[0])
    vu_copy = pltpu.make_async_copy(vu_hbm, vu, wsem.at[1])
    eg_copy = pltpu.make_async_copy(eg_hbm, eg, wsem.at[2])
    eu_copy = pltpu.make_async_copy(eu_hbm, eu, wsem.at[3])

    own_q.start()
    cache_copy(0).start()
    lanes = lax.broadcasted_iota(jnp.int32, chosen.shape[1:], 1)
    square = (routes.shape[1], routes.shape[1])
    diagonal = lax.broadcasted_iota(jnp.int32, square, 0) == lax.broadcasted_iota(jnp.int32, square, 1)
    named = jnp.zeros(lanes.shape, F32)
    for k in range(routes.shape[0]):
        choice = jnp.where(diagonal, routes[k : k + 1, :].astype(F32), 0.0)
        named = named + (jnp.sum(choice, axis=1, keepdims=True) == lanes.astype(F32)).astype(F32)
    chosen[e] = named

    barrier = pltpu.get_barrier_semaphore()
    for to in peers:
        pl.semaphore_signal(
            barrier, inc=1, device_id={"ctx": to[0], "exp": to[1]}, device_id_type=MESH
        )
    pl.semaphore_wait(barrier, len(peers))

    for g in range(AHEAD):
        for k in range(3):
            own_copy(g, k).start()
    for k in range(3):
        route_copy(k).start()
    vu_copy.start()
    own_q.wait()

    rows = 8 * heads_rows

    def attend(g):
        cache_copy(g).wait()

        @pl.when(g + 1 < chunks)
        def _():
            cache_copy(g + 1).start()

        first = lax.broadcasted_iota(jnp.int32, (heads_rows, 128), 1) < 64
        position = me * block_len + lax.broadcasted_iota(jnp.int32, (1, block_len), 1)
        for r in range(PAIR):
            q = qbuf[g, :, r].reshape(rows, width)
            sbuf[r] = jnp.dot(q, cbuf[g % 2, r], preferred_element_type=F32)
        for r in range(PAIR):
            length = lens[g * PAIR + r]
            bias = jnp.concatenate(
                [
                    jnp.broadcast_to(
                        jnp.where(position < length + j, 0.0, -1e30), (heads, block_len)
                    )
                    for j in range(2)
                ],
                axis=0,
            )
            for d in range(8):
                place = slice(d * heads_rows, (d + 1) * heads_rows)
                s = sbuf[r, place] + bias
                m = jnp.max(s, axis=1, keepdims=True)
                p = jnp.exp((s - m) * scale)
                total = jnp.sum(p, axis=1, keepdims=True)
                wbuf[r, place] = p.astype(BF16)
                m = m * scale
                z = jnp.where(m > -1e25, m + jnp.log(total), -1e30)
                mz[r, place] = jnp.where(first, jnp.where(m > -1e25, m, -1e30), z)
            acc[g % 2, r] = contract(wbuf[r], cbuf[g % 2, r, :latent], 1, 1)
            flat = jnp.transpose(mz[r])
            mown[g % 2, r : r + 1] = flat[0:1]
            stat[g, me, r : r + 1] = flat[64:65]
        for k in range(7):
            stat_copy(g, k).start()

    def normalise(g):
        for k in range(7):
            stat_copy(g, k).wait_recv()
        for r in range(PAIR):
            z = stat[g, :, r]
            top = jnp.max(z, axis=0, keepdims=True)
            whole = top + jnp.log(jnp.sum(jnp.exp(z - top), axis=0, keepdims=True))
            factor = jnp.exp(mown[g % 2, r : r + 1] - whole)
            factor = jnp.transpose(jnp.broadcast_to(factor, (128, rows)))
            for k in range(latent // 128):
                part = acc[g % 2, r, :, k * 128 : (k + 1) * 128] * factor
                norm[g, :, :, :, r, :, k * 128 : (k + 1) * 128] = part.astype(BF16).reshape(
                    2, 2, 2, heads_rows, 128
                )
        fold_copy(g).start()

    def fold(g):
        fold_copy(g).wait_recv()
        crx[g] = (crx[g].astype(F32) + norm[g, c].astype(F32)).astype(BF16)
        cross_copy(g, 0).start()
        cross_copy(g, 1).start()

    def cross(g):
        cross_copy(g, 0).wait_recv()
        x2[g] = (x2[g].astype(F32) + crx[g, :, ex, 0].astype(F32)).astype(BF16)
        last_copy(g, 0).start()
        cross_copy(g, 1).wait_recv()
        y2[g] = (y2[g].astype(F32) + crx[g, ey, :, 1].astype(F32)).astype(BF16)
        last_copy(g, 1).start()

    def last(g):
        last_copy(g, 0).wait_recv()
        ctx2[g % 2, 0] = (x2[g, ey].astype(F32) + y3[g].astype(F32)).astype(BF16)
        last_copy(g, 1).wait_recv()
        ctx2[g % 2, 1] = (y2[g, ex].astype(F32) + x3[g].astype(F32)).astype(BF16)

        @pl.when(g % 2 == 1)
        def _():
            both = ctx2[...].reshape(4 * heads_rows, latent)
            for h in range(heads):
                every = jnp.dot(both, vu[h], preferred_element_type=F32).reshape(8, heads, vdim)
                mine = lax.broadcasted_iota(jnp.int32, every.shape, 1) == h
                place = pl.ds(pl.multiple_of((g // 2) * 8, 8), 8)
                ho[place, h * vdim : (h + 1) * vdim] = jnp.sum(
                    jnp.where(mine, every, 0.0), axis=1
                )

    vu_copy.wait()

    def step(s, _):
        def at(lag, run):
            @pl.when((s >= lag) & (s < chunks + lag))
            def _():
                run(s - lag)

        def forward(g):
            own_copy(g, 1).wait_recv()
            diag_copy(g, 0).start()
            core_copy(g, 0).start()
            own_copy(g, 2).wait_recv()
            diag_copy(g, 1).start()
            core_copy(g, 1).start()

        def forward_diag(g):
            for k in range(2):
                diag_copy(g, k).wait_recv()
                core_copy(g, 2 + k).start()

        def attend_when_here(g):
            own_copy(g, 0).wait_recv()
            for k in range(4):
                core_copy(g, k).wait_recv()
            attend(g)

        at(0, forward)
        at(1, forward_diag)

        @pl.when(s + AHEAD < chunks)
        def _():
            for k in range(3):
                own_copy(s + AHEAD, k).start()

        at(3, normalise)
        at(4, fold)
        at(5, cross)
        at(6, last)
        at(2, attend_when_here)

        @pl.when(s < SLOTS)
        def _():
            op_copy(s).start()

        @pl.when(s == SLOTS)
        def _():
            eg_copy.start()

        @pl.when(s == SLOTS + 1)
        def _():
            eu_copy.start()

        return 0

    lax.fori_loop(0, chunks + 6, step, 0)

    own_rows = res.shape[0]

    def project(i, _):
        op_copy(i).wait()
        part = jnp.dot(ho[...].astype(BF16), wslot[i % SLOTS], preferred_element_type=F32)
        place = pl.ds(pl.multiple_of((i % per_half) * cols, cols), cols)
        pbuf[0, i // per_half, :, :, place] = part.astype(BF16).reshape(4, own_rows, cols)

        @pl.when(i + SLOTS < BLOCKS)
        def _():
            op_copy(i + SLOTS).start()

        @pl.when(i == per_half - 1)
        def _():
            swap_copy(0).start()

        return 0

    lax.fori_loop(0, BLOCKS, project, 0)
    for i in range(BLOCKS):
        down_copy(i).start()

    def reduce_rows(p):
        swap_copy(p).wait_recv()
        tsum[p] = (prx[p].astype(F32) + pbuf[p, 1].astype(F32)).astype(BF16)
        for k in (2, 0, 1):
            rows_copy(p, k).start()
        total = tsum[p, e].astype(F32)
        for k in range(3):
            rows_copy(p, k).wait_recv()
            total = total + rrx[p, k].astype(F32)
        return total

    own_cols = pl.ds(pl.multiple_of(c * half, half), half)
    hid[e, c] = (res[:, own_cols].astype(F32) + reduce_rows(0)).astype(BF16)
    for k in (2, 0, 1, 3):
        hid_copy(k).start()
    for k in range(3):
        hid_copy(k).wait_recv()
        hidfwd_copy(k).start()
    hid_copy(3).wait_recv()
    for k in range(3):
        hidfwd_copy(k).wait_recv()
        route_copy(k).wait_recv()
    eg_copy.wait()
    eu_copy.wait()

    sides = [hid[:, side].astype(F32).reshape(4 * own_rows, half) for side in range(2)]
    squares = sum(jnp.sum(v * v, axis=-1, keepdims=True) for v in sides)
    inverse = lax.rsqrt(squares / (2 * half) + 1e-06)
    for side in range(2):
        for k in range(half // 128):
            spread = gain[side * (half // 128) + k : side * (half // 128) + k + 1, :].astype(F32)
            piece = sides[side][:, k * 128 : (k + 1) * 128]
            xn[side, :, k * 128 : (k + 1) * 128] = (piece * inverse * spread).astype(BF16)
    span = [slice(side * half, (side + 1) * half) for side in range(2)]
    both_sides = lambda w: sum(
        jnp.dot(xn[side], w[span[side], :], preferred_element_type=F32) for side in range(2)
    )
    affinity = jax.nn.sigmoid(
        sum(contract(xn[side], router[:, span[side]], 1, 1) for side in range(2))
    )
    picked = affinity * chosen[...].reshape(4 * own_rows, 128)[:, : affinity.shape[1]]
    weights = route_scale * picked / jnp.sum(picked, axis=-1, keepdims=True)
    mine = lax.broadcasted_iota(jnp.int32, weights.shape, 1) == e
    gcol[...] = jnp.broadcast_to(
        jnp.sum(jnp.where(mine, weights, 0.0), axis=-1, keepdims=True), gcol.shape
    )
    gate_part = both_sides(eg)
    up_part = both_sides(eu)
    act[...] = (gate_part / (1.0 + jnp.exp(-gate_part)) * up_part).astype(BF16)

    for i in range(BLOCKS):
        down_copy(i).wait()
        block = wslot[3 + i // 4, (i % 4) * depth : (i % 4 + 1) * depth]
        part = jnp.dot(act[...], block, preferred_element_type=F32) * gcol[:, 0:1]
        place = slice((i % per_half) * cols, (i % per_half + 1) * cols)
        pbuf[1, i // per_half, :, :, place] = part.astype(BF16).reshape(4, own_rows, cols)
        if i == per_half - 1:
            swap_copy(1).start()
    out[...] = (hid[e, c].astype(F32) + reduce_rows(1)).astype(BF16)

    def drain(g, _):
        for k in range(3):
            own_copy(g, k).wait_send()
        for k in range(2):
            diag_copy(g, k).wait_send()
            cross_copy(g, k).wait_send()
            last_copy(g, k).wait_send()
        for k in range(4):
            core_copy(g, k).wait_send()
        for k in range(7):
            stat_copy(g, k).wait_send()
        fold_copy(g).wait_send()
        return 0

    lax.fori_loop(0, chunks, drain, 0)
    for k in range(3):
        route_copy(k).wait_send()
        hidfwd_copy(k).wait_send()
        rows_copy(0, k).wait_send()
        rows_copy(1, k).wait_send()
    for k in range(4):
        hid_copy(k).wait_send()
    for p in range(2):
        swap_copy(p).wait_send()


def fused_on_device(
    queries, latent_cache, context_lengths, value_up, out_proj, residual, norm_gain, router,
    routes, expert_gate, expert_up, expert_down,
):
    reqs, verify, heads, width = queries.shape
    chunks = reqs // PAIR
    hr = verify * heads
    _, block_len, _ = latent_cache.shape
    _, latent, vdim = value_up.shape
    own_rows, model = residual.shape
    half = model // 2
    ff = expert_down.shape[1]
    rows = 8 * hr
    _, count = lay_out(chunks)
    vmem, anywhere = pl.BlockSpec(memory_space=pltpu.VMEM), pl.BlockSpec(memory_space=pl.ANY)
    scratch = [
        pltpu.VMEM((chunks, 8, PAIR, hr, width), BF16),
        pltpu.VMEM((2, PAIR, width, block_len), BF16),
        pltpu.VMEM((2, PAIR, rows, latent), F32),
        pltpu.VMEM((2, PAIR, rows), F32),
        pltpu.VMEM((chunks, 8, PAIR, rows), F32),
        pltpu.VMEM((chunks, 2, 2, 2, PAIR, hr, latent), BF16),
        pltpu.VMEM((chunks, 2, 2, PAIR, hr, latent), BF16),
        pltpu.VMEM((chunks, 2, hr, latent), BF16),
        pltpu.VMEM((chunks, 2, hr, latent), BF16),
        pltpu.VMEM((chunks, hr, latent), BF16),
        pltpu.VMEM((chunks, hr, latent), BF16),
        pltpu.VMEM((2, PAIR, hr, latent), BF16),
        pltpu.VMEM((heads, latent, vdim), BF16),
        pltpu.VMEM((reqs * verify, heads * vdim), F32),
        pltpu.VMEM((SLOTS, heads * vdim, model // BLOCKS), BF16),
        pltpu.VMEM((model, ff), BF16),
        pltpu.VMEM((model, ff), BF16),
        pltpu.VMEM((PAIR, rows, block_len), F32),
        pltpu.VMEM((PAIR, rows, block_len), BF16),
        pltpu.VMEM((PAIR, rows, 128), F32),
        pltpu.VMEM((4, own_rows, 128), F32),
        pltpu.VMEM((2, 2, 4, own_rows, half), BF16),
        pltpu.VMEM((2, 4, own_rows, half), BF16),
        pltpu.VMEM((2, 4, own_rows, half), BF16),
        pltpu.VMEM((2, 3, own_rows, half), BF16),
        pltpu.VMEM((4, 2, own_rows, half), BF16),
        pltpu.VMEM((2, 4 * own_rows, half), BF16),
        pltpu.VMEM((4 * own_rows, ff), BF16),
        pltpu.VMEM((4 * own_rows, 128), F32),
        pltpu.SemaphoreType.DMA((count,)),
        pltpu.SemaphoreType.DMA((count,)),
        pltpu.SemaphoreType.DMA((2,)),
        pltpu.SemaphoreType.DMA((4 + BLOCKS,)),
        pltpu.SemaphoreType.DMA((SLOTS,)),
    ]
    return pl.pallas_call(
        layer_kernel,
        out_shape=jax.ShapeDtypeStruct((own_rows, half), BF16),
        in_specs=[pl.BlockSpec(memory_space=pltpu.SMEM)] + [anywhere] * 4 + [vmem] * 2
        + [vmem] * 2 + [anywhere] * 3,
        out_specs=vmem,
        scratch_shapes=scratch,
        compiler_params=pltpu.CompilerParams(
            collective_id=0, has_side_effects=True, vmem_limit_bytes=62 * 1024 * 1024
        ),
        cost_estimate=pl.CostEstimate(
            flops=6_000_000_000, bytes_accessed=64_000_000, transcendentals=2_000_000
        ),
    )(
        context_lengths,
        queries.reshape(chunks, PAIR, hr, width),
        jnp.swapaxes(latent_cache, 1, 2).reshape(chunks, PAIR, width, block_len),
        value_up,
        out_proj,
        residual,
        norm_gain.reshape(model // 128, 128),
        router.T,
        routes.T,
        expert_gate[0],
        expert_up[0],
        expert_down[0],
    )


def solution(mesh):
    grouped = mesh.shape["ctx"] == 2 and mesh.shape["exp"] == 4
    body = fused_on_device if grouped else on_device
    return jax.shard_map(
        body,
        mesh=mesh,
        in_specs=(
            P("req", None, ("ctx", "exp"), None),
            P("req", ("ctx", "exp"), None),
            P("req"),
            P(("ctx", "exp"), None, None),
            P(("ctx", "exp"), None),
            P(("req", "exp"), None),
            P(),
            P(),
            P(("req", "exp"), None),
            P("exp", None, "ctx"),
            P("exp", None, "ctx"),
            P("exp", "ctx", None),
        ),
        out_specs=P(("req", "exp"), "ctx"),
        check_vma=False,
    )
```

profile of v0, /device:TPU:0, one launch (start us, length us, event | category | flops | bytes accessed | tf_op | source)
XLA Modules:
  0.0 96.6 jit_solution(5481486874766711608)
XLA Ops:
  0.0 95.2 %shard_map.118 = bf16[8,3584]{1,0:T(8,128)(2,1)} custom-call(s32[16]{0:T(128)} %lens.1, bf16[8,2,32,576]{3,2,1,0:T(8,128)(2,1)} %bitcast.14, bf16[8,2,576,512]{3,2,1,0:T(8,128)(2,1)} %bitcast.10, bf16[16,512,128]{2,1,0:T(8,128)(2,1)} %vu_hbm.1, bf16[2048,7168]{1,0:T(8,128)(2,1)} %op_hbm.1, bf16[8,7168]{1,0:T(8,128)(2,1)} %res.1, bf16[56,128]{1,0:T(8,128)(2,1)} %bitcast.16, ...), custom_call_target="tpu_custom_call" | custom-call | flops 6000000000 | bytes 64000000 | tf_op jit(solution)/shard_map/pallas_call | solution.py:584
  95.2 1.4 %copy.14 = bf16[8,3584]{1,0:T(8,128)(2,1)} copy(bf16[8,3584]{1,0:T(8,128)(2,1)} %shard_map.118) | data formatting | bytes 114688
where the time goes:
time: 96.8 us; the launch traced here: 96.6 us
  Pallas kernels  95.2 us (98%)
  local copies, waits for them, and re-layouts  1.45 us (1%)
    pallas_call x1, Pallas kernels, fused_on_device(): pl.pallas_call(layer_kernel, out_shape=jax.ShapeDtypeStruct((own_rows, ha...  95.2 us

commit v1 on v0

--- a/solution.py
+++ b/solution.py
@@ -400,10 +400,10 @@
             for k in range(3):
                 own_copy(s + AHEAD, k).start()
 
-        at(3, normalise)
-        at(4, fold)
-        at(5, cross)
-        at(6, last)
+        at(4, normalise)
+        at(5, fold)
+        at(6, cross)
+        at(7, last)
         at(2, attend_when_here)
 
         @pl.when(s < SLOTS)
@@ -420,7 +420,7 @@
 
         return 0
 
-    lax.fori_loop(0, chunks + 6, step, 0)
+    lax.fori_loop(0, chunks + 7, step, 0)
 
     own_rows = res.shape[0]
 

time: 96.8 us -> 82.1 us (0.85)
  Pallas kernels: 95.2 us -> 80.4 us
    pallas_call x1, Pallas kernels: 95.2 us -> 80.4 us  [fused_on_device(): pl.pallas_call(layer_kernel, out_shape=jax.ShapeDtypeStruct((own_rows, ha...]
where the time goes in v1:
time: 82.1 us; the launch traced here: 81.9 us
  Pallas kernels  80.4 us (98%)
  local copies, waits for them, and re-layouts  1.45 us (2%)
    pallas_call x1, Pallas kernels, fused_on_device(): pl.pallas_call(layer_kernel, out_shape=jax.ShapeDtypeStruct((own_rows, ha...  80.4 us

profile of v1, /device:TPU:0, one launch (start us, length us, event | category | flops | bytes accessed | tf_op | source)
XLA Modules:
  0.0 81.9 jit_solution(3037585097146976802)
XLA Ops:
  0.0 80.4 %shard_map.118 = bf16[8,3584]{1,0:T(8,128)(2,1)} custom-call(s32[16]{0:T(128)} %lens.1, bf16[8,2,32,576]{3,2,1,0:T(8,128)(2,1)} %bitcast.14, bf16[8,2,576,512]{3,2,1,0:T(8,128)(2,1)} %bitcast.10, bf16[16,512,128]{2,1,0:T(8,128)(2,1)} %vu_hbm.1, bf16[2048,7168]{1,0:T(8,128)(2,1)} %op_hbm.1, bf16[8,7168]{1,0:T(8,128)(2,1)} %res.1, bf16[56,128]{1,0:T(8,128)(2,1)} %bitcast.16, ...), custom_call_target="tpu_custom_call" | custom-call | flops 6000000000 | bytes 64000000 | tf_op jit(solution)/shard_map/pallas_call | solution.py:584
  80.4 1.4 %copy.14 = bf16[8,3584]{1,0:T(8,128)(2,1)} copy(bf16[8,3584]{1,0:T(8,128)(2,1)} %shard_map.118) | data formatting | bytes 114688

commit v2 on v1

--- a/solution.py
+++ b/solution.py
@@ -123,6 +123,7 @@
 PAIR = 2
 SLOTS = 5
 BLOCKS = 8
+PIECES = 2
 AHEAD = 3
 
 
@@ -133,7 +134,10 @@
     ):
         places[name] = (count, number)
         count += number * chunks
-    for name, number in (("route", 3), ("swap", 2), ("rows", 6), ("hid", 4), ("hidfwd", 3)):
+    for name, number in (
+        ("route", 3), ("swap", 2 * PIECES), ("rows", 6 * PIECES), ("hid", 4 * PIECES),
+        ("hidfwd", 3 * PIECES),
+    ):
         places[name] = (count, number)
         count += number
     return places, count
@@ -147,7 +151,7 @@
     lens, q_hbm, cache_hbm, vu_hbm, op_hbm, res, gain, router, routes, eg_hbm, eu_hbm, ed_hbm,
     out,
     qbuf, cbuf, acc, mown, stat, norm, crx, x2, y2, x3, y3, ctx2, vu, ho, wslot, eg, eu,
-    sbuf, wbuf, mz, chosen, pbuf, prx, tsum, rrx, hid, xn, act, gcol,
+    sbuf, wbuf, mz, spread, chosen, pbuf, prx, tsum, rrx, hid, xn, act, gcol,
     send, recv, csem, wsem, osem,
 ):
     chunks, _, heads_rows, width = q_hbm.shape
@@ -156,7 +160,8 @@
     vdim = vu.shape[2]
     places, _ = lay_out(chunks)
     scale = 1.0 / math.sqrt(vdim + width - latent)
-    half = hid.shape[3]
+    piece = hid.shape[4]
+    half = piece * PIECES
     cols = half * 2 // BLOCKS
     per_half = BLOCKS // 2
     c = lax.axis_index("ctx")
@@ -211,19 +216,22 @@
     def route_copy(k):
         return remote("route", 0, k, chosen.at[e], chosen.at[e], (c, others[k]))
 
-    def swap_copy(p):
-        return remote("swap", 0, p, pbuf.at[p, 0], prx.at[p], core_to)
-
-    def rows_copy(p, k):
-        return remote("rows", 0, p * 3 + k, tsum.at[p, others[k]], rrx.at[p, k], (c, others[k]))
-
-    def hid_copy(k):
+    def swap_copy(p, j):
+        return remote("swap", 0, p * PIECES + j, pbuf.at[p, 0, j], prx.at[p, j], core_to)
+
+    def rows_copy(p, j, k):
+        return remote(
+            "rows", 0, (p * PIECES + j) * 3 + k, tsum.at[p, j, others[k]], rrx.at[p, j, k],
+            (c, others[k]),
+        )
+
+    def hid_copy(j, k):
         to = (x_to, y_to, (c, ed_n), core_to)[k]
-        return remote("hid", 0, k, hid.at[e, c], hid.at[e, c], to)
-
-    def hidfwd_copy(k):
-        view = hid.at[others[k], c]
-        return remote("hidfwd", 0, k, view, view, core_to)
+        return remote("hid", 0, j * 4 + k, hid.at[c, j, e], hid.at[c, j, e], to)
+
+    def hidfwd_copy(j, k):
+        view = hid.at[c, j, others[k]]
+        return remote("hidfwd", 0, j * 3 + k, view, view, core_to)
 
     def cache_copy(g):
         return pltpu.make_async_copy(cache_hbm.at[g], cbuf.at[g % 2], csem.at[g % 2])
@@ -274,6 +282,9 @@
     for k in range(3):
         route_copy(k).start()
     vu_copy.start()
+    lanes_of = piece // 128
+    for i in range(2 * PIECES):
+        spread[i] = gain[i * lanes_of : (i + 1) * lanes_of, :].astype(F32)
     own_q.wait()
 
     rows = 8 * heads_rows
@@ -424,85 +435,86 @@
 
     own_rows = res.shape[0]
 
-    def project(i, _):
+    per_piece = per_half // PIECES
+
+    def put(p, i, part):
+        place = slice(i % per_piece * cols, (i % per_piece + 1) * cols)
+        j = i % per_half // per_piece
+        pbuf[p, i // per_half, j, :, :, place] = part.astype(BF16).reshape(4, own_rows, cols)
+        if i % per_piece == per_piece - 1:
+            if i < per_half:
+                swap_copy(p, j).start()
+            else:
+                swap_copy(p, j).wait_recv()
+                total = prx[p, j].astype(F32) + pbuf[p, 1, j].astype(F32)
+                tsum[p, j] = total.astype(BF16)
+                for k in (2, 0, 1):
+                    rows_copy(p, j, k).start()
+
+    def rows_total(p, j):
+        total = tsum[p, j, e].astype(F32)
+        for k in range(3):
+            rows_copy(p, j, k).wait_recv()
+            total = total + rrx[p, j, k].astype(F32)
+        return total
+
+    head_out = ho[...].astype(BF16)
+    for i in range(BLOCKS):
         op_copy(i).wait()
-        part = jnp.dot(ho[...].astype(BF16), wslot[i % SLOTS], preferred_element_type=F32)
-        place = pl.ds(pl.multiple_of((i % per_half) * cols, cols), cols)
-        pbuf[0, i // per_half, :, :, place] = part.astype(BF16).reshape(4, own_rows, cols)
-
-        @pl.when(i + SLOTS < BLOCKS)
-        def _():
+        put(0, i, jnp.dot(head_out, wslot[i % SLOTS], preferred_element_type=F32))
+        if i + SLOTS < BLOCKS:
             op_copy(i + SLOTS).start()
-
-        @pl.when(i == per_half - 1)
-        def _():
-            swap_copy(0).start()
-
-        return 0
-
-    lax.fori_loop(0, BLOCKS, project, 0)
     for i in range(BLOCKS):
         down_copy(i).start()
 
-    def reduce_rows(p):
-        swap_copy(p).wait_recv()
-        tsum[p] = (prx[p].astype(F32) + pbuf[p, 1].astype(F32)).astype(BF16)
-        for k in (2, 0, 1):
-            rows_copy(p, k).start()
-        total = tsum[p, e].astype(F32)
-        for k in range(3):
-            rows_copy(p, k).wait_recv()
-            total = total + rrx[p, k].astype(F32)
-        return total
-
-    own_cols = pl.ds(pl.multiple_of(c * half, half), half)
-    hid[e, c] = (res[:, own_cols].astype(F32) + reduce_rows(0)).astype(BF16)
-    for k in (2, 0, 1, 3):
-        hid_copy(k).start()
-    for k in range(3):
-        hid_copy(k).wait_recv()
-        hidfwd_copy(k).start()
-    hid_copy(3).wait_recv()
-    for k in range(3):
-        hidfwd_copy(k).wait_recv()
-        route_copy(k).wait_recv()
+    for j in range(PIECES):
+        own_cols = pl.ds(pl.multiple_of(c * half + j * piece, piece), piece)
+        hid[c, j, e] = (res[:, own_cols].astype(F32) + rows_total(0, j)).astype(BF16)
+        for k in (2, 0, 1, 3):
+            hid_copy(j, k).start()
     eg_copy.wait()
     eu_copy.wait()
 
-    sides = [hid[:, side].astype(F32).reshape(4 * own_rows, half) for side in range(2)]
-    squares = sum(jnp.sum(v * v, axis=-1, keepdims=True) for v in sides)
+    squares, logits, gate_part, up_part = 0.0, 0.0, 0.0, 0.0
+    for i in range(2 * PIECES):
+        side, j = (c if i < PIECES else 1 - c), i % PIECES
+        if i < PIECES:
+            for k in range(3):
+                hid_copy(j, k).wait_recv()
+                hidfwd_copy(j, k).start()
+        else:
+            hid_copy(j, 3).wait_recv()
+            for k in range(3):
+                hidfwd_copy(j, k).wait_recv()
+        wide = hid[side, j].astype(F32).reshape(4 * own_rows, piece)
+        squares = squares + jnp.sum(wide * wide, axis=-1, keepdims=True)
+        for k in range(piece // 128):
+            lane = slice(k * 128, (k + 1) * 128)
+            xn[i, :, lane] = (wide[:, lane] * spread[side * PIECES + j, k : k + 1]).astype(BF16)
+        span = pl.ds(pl.multiple_of(side * half + j * piece, piece), piece)
+        logits = logits + contract(xn[i], router[:, span], 1, 1)
+        gate_part = gate_part + jnp.dot(xn[i], eg[span, :], preferred_element_type=F32)
+        up_part = up_part + jnp.dot(xn[i], eu[span, :], preferred_element_type=F32)
     inverse = lax.rsqrt(squares / (2 * half) + 1e-06)
-    for side in range(2):
-        for k in range(half // 128):
-            spread = gain[side * (half // 128) + k : side * (half // 128) + k + 1, :].astype(F32)
-            piece = sides[side][:, k * 128 : (k + 1) * 128]
-            xn[side, :, k * 128 : (k + 1) * 128] = (piece * inverse * spread).astype(BF16)
-    span = [slice(side * half, (side + 1) * half) for side in range(2)]
-    both_sides = lambda w: sum(
-        jnp.dot(xn[side], w[span[side], :], preferred_element_type=F32) for side in range(2)
-    )
-    affinity = jax.nn.sigmoid(
-        sum(contract(xn[side], router[:, span[side]], 1, 1) for side in range(2))
-    )
+    gate_part, up_part = gate_part * inverse, up_part * inverse
+    act[...] = (gate_part / (1.0 + jnp.exp(-gate_part)) * up_part).astype(BF16)
+    for k in range(3):
+        route_copy(k).wait_recv()
+    affinity = jax.nn.sigmoid(logits * inverse)
     picked = affinity * chosen[...].reshape(4 * own_rows, 128)[:, : affinity.shape[1]]
     weights = route_scale * picked / jnp.sum(picked, axis=-1, keepdims=True)
     mine = lax.broadcasted_iota(jnp.int32, weights.shape, 1) == e
     gcol[...] = jnp.broadcast_to(
         jnp.sum(jnp.where(mine, weights, 0.0), axis=-1, keepdims=True), gcol.shape
     )
-    gate_part = both_sides(eg)
-    up_part = both_sides(eu)
-    act[...] = (gate_part / (1.0 + jnp.exp(-gate_part)) * up_part).astype(BF16)
 
     for i in range(BLOCKS):
         down_copy(i).wait()
         block = wslot[3 + i // 4, (i % 4) * depth : (i % 4 + 1) * depth]
-        part = jnp.dot(act[...], block, preferred_element_type=F32) * gcol[:, 0:1]
-        place = slice((i % per_half) * cols, (i % per_half + 1) * cols)
-        pbuf[1, i // per_half, :, :, place] = part.astype(BF16).reshape(4, own_rows, cols)
-        if i == per_half - 1:
-            swap_copy(1).start()
-    out[...] = (hid[e, c].astype(F32) + reduce_rows(1)).astype(BF16)
+        put(1, i, jnp.dot(act[...], block, preferred_element_type=F32) * gcol[:, 0:1])
+    for j in range(PIECES):
+        total = hid[c, j, e].astype(F32) + rows_total(1, j)
+        out[:, j * piece : (j + 1) * piece] = total.astype(BF16)
 
     def drain(g, _):
         for k in range(3):
@@ -521,13 +533,15 @@
     lax.fori_loop(0, chunks, drain, 0)
     for k in range(3):
         route_copy(k).wait_send()
-        hidfwd_copy(k).wait_send()
-        rows_copy(0, k).wait_send()
-        rows_copy(1, k).wait_send()
-    for k in range(4):
-        hid_copy(k).wait_send()
-    for p in range(2):
-        swap_copy(p).wait_send()
+        for j in range(PIECES):
+            hidfwd_copy(j, k).wait_send()
+            rows_copy(0, j, k).wait_send()
+            rows_copy(1, j, k).wait_send()
+    for j in range(PIECES):
+        for k in range(4):
+            hid_copy(j, k).wait_send()
+        for p in range(2):
+            swap_copy(p, j).wait_send()
 
 
 def fused_on_device(
@@ -541,6 +555,7 @@
     _, latent, vdim = value_up.shape
     own_rows, model = residual.shape
     half = model // 2
+    piece = half // PIECES
     ff = expert_down.shape[1]
     rows = 8 * hr
     _, count = lay_out(chunks)
@@ -566,13 +581,14 @@
         pltpu.VMEM((PAIR, rows, block_len), F32),
         pltpu.VMEM((PAIR, rows, block_len), BF16),
         pltpu.VMEM((PAIR, rows, 128), F32),
+        pltpu.VMEM((2 * PIECES, piece // 128, 128), F32),
         pltpu.VMEM((4, own_rows, 128), F32),
-        pltpu.VMEM((2, 2, 4, own_rows, half), BF16),
-        pltpu.VMEM((2, 4, own_rows, half), BF16),
-        pltpu.VMEM((2, 4, own_rows, half), BF16),
-        pltpu.VMEM((2, 3, own_rows, half), BF16),
-        pltpu.VMEM((4, 2, own_rows, half), BF16),
-        pltpu.VMEM((2, 4 * own_rows, half), BF16),
+        pltpu.VMEM((2, 2, PIECES, 4, own_rows, piece), BF16),
+        pltpu.VMEM((2, PIECES, 4, own_rows, piece), BF16),
+        pltpu.VMEM((2, PIECES, 4, own_rows, piece), BF16),
+        pltpu.VMEM((2, PIECES, 3, own_rows, piece), BF16),
+        pltpu.VMEM((2, PIECES, 4, own_rows, piece), BF16),
+        pltpu.VMEM((2 * PIECES, 4 * own_rows, piece), BF16),
         pltpu.VMEM((4 * own_rows, ff), BF16),
         pltpu.VMEM((4 * own_rows, 128), F32),
         pltpu.SemaphoreType.DMA((count,)),

time: 82.1 us -> 80.5 us (0.981)
  Pallas kernels: 80.4 us -> 78.8 us
    pallas_call x1, Pallas kernels: 80.4 us -> 78.8 us  [fused_on_device(): pl.pallas_call(layer_kernel, out_shape=jax.ShapeDtypeStruct((own_rows, ha...]
where the time goes in v2:
time: 80.5 us; the launch traced here: 80.3 us
  Pallas kernels  78.8 us (98%)
  local copies, waits for them, and re-layouts  1.45 us (2%)
    pallas_call x1, Pallas kernels, fused_on_device(): pl.pallas_call(layer_kernel, out_shape=jax.ShapeDtypeStruct((own_rows, ha...  78.8 us

profile of v2, /device:TPU:0, one launch (start us, length us, event | category | flops | bytes accessed | tf_op | source)
XLA Modules:
  0.0 80.3 jit_solution(2574861989318414834)
XLA Ops:
  0.0 78.8 %shard_map.118 = bf16[8,3584]{1,0:T(8,128)(2,1)} custom-call(s32[16]{0:T(128)} %lens.1, bf16[8,2,32,576]{3,2,1,0:T(8,128)(2,1)} %bitcast.14, bf16[8,2,576,512]{3,2,1,0:T(8,128)(2,1)} %bitcast.10, bf16[16,512,128]{2,1,0:T(8,128)(2,1)} %vu_hbm.1, bf16[2048,7168]{1,0:T(8,128)(2,1)} %op_hbm.1, bf16[8,7168]{1,0:T(8,128)(2,1)} %res.1, bf16[56,128]{1,0:T(8,128)(2,1)} %bitcast.16, ...), custom_call_target="tpu_custom_call" | custom-call | flops 6000000000 | bytes 64000000 | tf_op jit(solution)/shard_map/pallas_call | solution.py:600
  78.8 1.4 %copy.14 = bf16[8,3584]{1,0:T(8,128)(2,1)} copy(bf16[8,3584]{1,0:T(8,128)(2,1)} %shard_map.118) | data formatting | bytes 114688

commit v3 on v2

--- a/solution.py
+++ b/solution.py
@@ -121,10 +121,10 @@
 F32 = jnp.float32
 BF16 = jnp.bfloat16
 PAIR = 2
-SLOTS = 5
-BLOCKS = 8
+SLOTS = 3
+BLOCKS = 4
 PIECES = 2
-AHEAD = 3
+AHEAD = 2
 
 
 def lay_out(chunks):
@@ -150,7 +150,7 @@
 def layer_kernel(
     lens, q_hbm, cache_hbm, vu_hbm, op_hbm, res, gain, router, routes, eg_hbm, eu_hbm, ed_hbm,
     out,
-    qbuf, cbuf, acc, mown, stat, norm, crx, x2, y2, x3, y3, ctx2, vu, ho, wslot, eg, eu,
+    qbuf, cbuf, acc, mown, stat, norm, crx, x2, y2, x3, y3, ctx2, vu, ho, wslot, eg,
     sbuf, wbuf, mz, spread, chosen, pbuf, prx, tsum, rrx, hid, xn, act, gcol,
     send, recv, csem, wsem, osem,
 ):
@@ -248,15 +248,28 @@
     depth = ed_hbm.shape[0]
 
     def down_copy(i):
-        place = pl.ds(pl.multiple_of((i % 4) * depth, depth), depth)
+        place = pl.ds(i * depth, depth)
         return pltpu.make_async_copy(
-            ed_hbm.at[:, pl.ds(column(i), cols)], wslot.at[3 + i // 4, place], wsem.at[4 + i]
+            ed_hbm.at[:, pl.ds(column(i), cols)], wslot.at[1, place], wsem.at[4 + i]
         )
 
     own_q = pltpu.make_async_copy(q_hbm, qbuf.at[:, me], wsem.at[0])
     vu_copy = pltpu.make_async_copy(vu_hbm, vu, wsem.at[1])
     eg_copy = pltpu.make_async_copy(eg_hbm, eg, wsem.at[2])
-    eu_copy = pltpu.make_async_copy(eu_hbm, eu, wsem.at[3])
+
+    def part_of(i):
+        side, j = (c if i < PIECES else 1 - c), i % PIECES
+        return side, j, pl.ds(pl.multiple_of(side * half + j * piece, piece), piece)
+
+    def up_place(i):
+        width = eu_hbm.shape[1]
+        return wslot.at[2 if i < 3 else 0, 0:piece, i % 3 * width : (i % 3 + 1) * width]
+
+    def up_copy(i):
+        return pltpu.make_async_copy(
+            eu_hbm.at[part_of(i)[2], :], up_place(i), wsem.at[4 + BLOCKS + i]
+        )
+
 
     own_q.start()
     cache_copy(0).start()
@@ -322,12 +335,13 @@
                 m = m * scale
                 z = jnp.where(m > -1e25, m + jnp.log(total), -1e30)
                 mz[r, place] = jnp.where(first, jnp.where(m > -1e25, m, -1e30), z)
-            acc[g % 2, r] = contract(wbuf[r], cbuf[g % 2, r, :latent], 1, 1)
             flat = jnp.transpose(mz[r])
             mown[g % 2, r : r + 1] = flat[0:1]
             stat[g, me, r : r + 1] = flat[64:65]
         for k in range(7):
             stat_copy(g, k).start()
+        for r in range(PAIR):
+            acc[g % 2, r] = contract(wbuf[r], cbuf[g % 2, r, :latent], 1, 1)
 
     def normalise(g):
         for k in range(7):
@@ -425,10 +439,6 @@
         def _():
             eg_copy.start()
 
-        @pl.when(s == SLOTS + 1)
-        def _():
-            eu_copy.start()
-
         return 0
 
     lax.fori_loop(0, chunks + 7, step, 0)
@@ -464,8 +474,12 @@
         put(0, i, jnp.dot(head_out, wslot[i % SLOTS], preferred_element_type=F32))
         if i + SLOTS < BLOCKS:
             op_copy(i + SLOTS).start()
-    for i in range(BLOCKS):
-        down_copy(i).start()
+        if i == 1:
+            for k in range(BLOCKS):
+                down_copy(k).start()
+        if i >= 2:
+            for k in range(3) if i == 2 else (3,):
+                up_copy(k).start()
 
     for j in range(PIECES):
         own_cols = pl.ds(pl.multiple_of(c * half + j * piece, piece), piece)
@@ -473,11 +487,10 @@
         for k in (2, 0, 1, 3):
             hid_copy(j, k).start()
     eg_copy.wait()
-    eu_copy.wait()
 
     squares, logits, gate_part, up_part = 0.0, 0.0, 0.0, 0.0
     for i in range(2 * PIECES):
-        side, j = (c if i < PIECES else 1 - c), i % PIECES
+        side, j, span = part_of(i)
         if i < PIECES:
             for k in range(3):
                 hid_copy(j, k).wait_recv()
@@ -491,10 +504,10 @@
         for k in range(piece // 128):
             lane = slice(k * 128, (k + 1) * 128)
             xn[i, :, lane] = (wide[:, lane] * spread[side * PIECES + j, k : k + 1]).astype(BF16)
-        span = pl.ds(pl.multiple_of(side * half + j * piece, piece), piece)
         logits = logits + contract(xn[i], router[:, span], 1, 1)
         gate_part = gate_part + jnp.dot(xn[i], eg[span, :], preferred_element_type=F32)
-        up_part = up_part + jnp.dot(xn[i], eu[span, :], preferred_element_type=F32)
+        up_copy(i).wait()
+        up_part = up_part + jnp.dot(xn[i], up_place(i)[...], preferred_element_type=F32)
     inverse = lax.rsqrt(squares / (2 * half) + 1e-06)
     gate_part, up_part = gate_part * inverse, up_part * inverse
     act[...] = (gate_part / (1.0 + jnp.exp(-gate_part)) * up_part).astype(BF16)
@@ -510,7 +523,7 @@
 
     for i in range(BLOCKS):
         down_copy(i).wait()
-        block = wslot[3 + i // 4, (i % 4) * depth : (i % 4 + 1) * depth]
+        block = wslot[1, i * depth : (i + 1) * depth]
         put(1, i, jnp.dot(act[...], block, preferred_element_type=F32) * gcol[:, 0:1])
     for j in range(PIECES):
         total = hid[c, j, e].astype(F32) + rows_total(1, j)
@@ -577,7 +590,6 @@
         pltpu.VMEM((reqs * verify, heads * vdim), F32),
         pltpu.VMEM((SLOTS, heads * vdim, model // BLOCKS), BF16),
         pltpu.VMEM((model, ff), BF16),
-        pltpu.VMEM((model, ff), BF16),
         pltpu.VMEM((PAIR, rows, block_len), F32),
         pltpu.VMEM((PAIR, rows, block_len), BF16),
         pltpu.VMEM((PAIR, rows, 128), F32),
@@ -594,7 +606,7 @@
         pltpu.SemaphoreType.DMA((count,)),
         pltpu.SemaphoreType.DMA((count,)),
         pltpu.SemaphoreType.DMA((2,)),
-        pltpu.SemaphoreType.DMA((4 + BLOCKS,)),
+        pltpu.SemaphoreType.DMA((4 + BLOCKS + 2 * PIECES,)),
         pltpu.SemaphoreType.DMA((SLOTS,)),
     ]
     return pl.pallas_call(

time: 80.5 us -> 80.3 us (level)
  no operation moved by 1% of the time
where the time goes in v3:
time: 80.3 us; the launch traced here: 80.1 us
  Pallas kernels  78.6 us (98%)
  local copies, waits for them, and re-layouts  1.45 us (2%)
    pallas_call x1, Pallas kernels, fused_on_device(): pl.pallas_call(layer_kernel, out_shape=jax.ShapeDtypeStruct((own_rows, ha...  78.6 us

profile of v3, /device:TPU:0, one launch (start us, length us, event | category | flops | bytes accessed | tf_op | source)
XLA Modules:
  0.0 80.1 jit_solution(6467644048107418621)
XLA Ops:
  0.0 78.6 %shard_map.118 = bf16[8,3584]{1,0:T(8,128)(2,1)} custom-call(s32[16]{0:T(128)} %lens.1, bf16[8,2,32,576]{3,2,1,0:T(8,128)(2,1)} %bitcast.14, bf16[8,2,576,512]{3,2,1,0:T(8,128)(2,1)} %bitcast.10, bf16[16,512,128]{2,1,0:T(8,128)(2,1)} %vu_hbm.1, bf16[2048,7168]{1,0:T(8,128)(2,1)} %op_hbm.1, bf16[8,7168]{1,0:T(8,128)(2,1)} %res.1, bf16[56,128]{1,0:T(8,128)(2,1)} %bitcast.16, ...), custom_call_target="tpu_custom_call" | custom-call | flops 6000000000 | bytes 64000000 | tf_op jit(solution)/shard_map/pallas_call | solution.py:612
  78.7 1.4 %copy.14 = bf16[8,3584]{1,0:T(8,128)(2,1)} copy(bf16[8,3584]{1,0:T(8,128)(2,1)} %shard_map.118) | data formatting | bytes 114688

commit v4 on v3

--- a/solution.py
+++ b/solution.py
@@ -420,15 +420,16 @@
         at(0, forward)
         at(1, forward_diag)
 
+        at(4, normalise)
+        at(5, fold)
+        at(6, cross)
+        at(7, last)
+
         @pl.when(s + AHEAD < chunks)
         def _():
             for k in range(3):
                 own_copy(s + AHEAD, k).start()
 
-        at(4, normalise)
-        at(5, fold)
-        at(6, cross)
-        at(7, last)
         at(2, attend_when_here)
 
         @pl.when(s < SLOTS)

time: 80.3 us -> 80.1 us (level)
  no operation moved by 1% of the time
where the time goes in v4:
time: 80.1 us; the launch traced here: 79.8 us
  Pallas kernels  78.4 us (98%)
  local copies, waits for them, and re-layouts  1.45 us (2%)
    pallas_call x1, Pallas kernels, fused_on_device(): pl.pallas_call(layer_kernel, out_shape=jax.ShapeDtypeStruct((own_rows, ha...  78.4 us

profile of v4, /device:TPU:0, one launch (start us, length us, event | category | flops | bytes accessed | tf_op | source)
XLA Modules:
  0.0 79.8 jit_solution(1835048237520840290)
XLA Ops:
  0.0 78.4 %shard_map.118 = bf16[8,3584]{1,0:T(8,128)(2,1)} custom-call(s32[16]{0:T(128)} %lens.1, bf16[8,2,32,576]{3,2,1,0:T(8,128)(2,1)} %bitcast.14, bf16[8,2,576,512]{3,2,1,0:T(8,128)(2,1)} %bitcast.10, bf16[16,512,128]{2,1,0:T(8,128)(2,1)} %vu_hbm.1, bf16[2048,7168]{1,0:T(8,128)(2,1)} %op_hbm.1, bf16[8,7168]{1,0:T(8,128)(2,1)} %res.1, bf16[56,128]{1,0:T(8,128)(2,1)} %bitcast.16, ...), custom_call_target="tpu_custom_call" | custom-call | flops 6000000000 | bytes 64000000 | tf_op jit(solution)/shard_map/pallas_call | solution.py:613
  78.4 1.4 %copy.14 = bf16[8,3584]{1,0:T(8,128)(2,1)} copy(bf16[8,3584]{1,0:T(8,128)(2,1)} %shard_map.118) | data formatting | bytes 114688
